TPU v7x, 512 devices: a whole 4x4x16 slice. The times are simulated.
512 devices in a mesh: space: 32 (over z_lo, x), sub: 16 (over z_hi, y, core).
Axes of the slice: x: 4, y: 4, z: 16 (z_hi: 2, z_lo: 8; z = z_hi * 8 + z_lo), core: 2. Of those that a mesh axis runs over, the one named last changes fastest.
Arguments:
- parent_local: bfloat16 [32, 64, 128], P('space'), may hold values from -6 to 6
- poles_mid: bfloat16 [512, 64, 128], P(('space', 'sub')), may hold values from -6 to 6
- poles_fine: bfloat16 [4096, 64, 128], P(('space', 'sub')), may hold values from -6 to 6
- transfer_mid: bfloat16 [189, 64, 64], replicated, may hold values from -0.125 to 0.125
- transfer_fine: bfloat16 [189, 64, 64], replicated, may hold values from -0.0546875 to 0.0546875
- shift_child: bfloat16 [8, 64, 64], replicated, may hold values from -0.75 to 0.75
- lists_mid: int32 [512, 189], P(('space', 'sub')), may hold values from -1 to 511, as said below
- lists_fine: int32 [4096, 189], P(('space', 'sub')), may hold values from -1 to 4095, as said below
- octant_mid: int32 [512], P(('space', 'sub')), may hold values from 0 to 7
- octant_fine: int32 [4096], P(('space', 'sub')), may hold values from 0 to 7
- parent_fine: int32 [4096], P(('space', 'sub')), may hold values from 0 to 511, as said below
Outputs:
- local_fine: bfloat16 [4096, 64, 128], P(('space', 'sub'))
Inputs may be any that keep to these rules, and one draw needn't show every extreme that they name: `lists_mid`: the sources named in the list of a level-4 box are distinct, differ from the box itself, and lie in its partition or in the partition just before or after it; a partition holds 16 consecutive level-4 boxes. A list names at least half of min(189, 47), rounded down, sources and at most all the sources it may use. `lists_fine`: the sources named in the list of a level-5 box are distinct, differ from the box itself, and lie in its partition or in the partition just before or after it; a partition holds 128 consecutive level-5 boxes. A list names at least half of min(189, 383), rounded down, sources and at most all the sources it may use. `parent_fine`: each level-4 box is the parent of exactly 8 level-5 boxes, all in its own partition.
All inputs are finite; a program needn't handle non-finite values.
Results may differ from a plain program's by a relative error of at most 0.0045.
Values may be sent and summed in bfloat16 or wider, within the bound.
A program may use at most 128 MiB of HBM per device.

v0:
```python
import math

import jax
import jax.numpy as jnp
from jax import lax
from jax.sharding import PartitionSpec as P


def padded(block, sides, width):
    for axis, dim in sides:
        count = lax.axis_size(axis)
        forward = [(i, i + 1) for i in range(count - 1)]
        backward = [(target, source) for source, target in forward]
        low = lax.ppermute(
            lax.slice_in_dim(block, block.shape[dim] - width, None, axis=dim), axis, forward
        )
        high = lax.ppermute(lax.slice_in_dim(block, 0, width, axis=dim), axis, backward)
        block = jnp.concatenate([low, block, high], axis=dim)
    return block


def far_field(operators, window, lists, offset):
    box_count = lists.shape[0]
    stride = math.gcd(box_count, 4)
    local_ids = jnp.where(lists >= 0, lists - offset, -1)

    def translate_block(entries):
        present = entries >= 0
        picked = window[jnp.where(present, entries, 0)]
        picked = jnp.where(present[:, :, None, None], picked, jnp.zeros((), window.dtype))
        return jnp.einsum("cij,gcjn->gin", operators, picked, preferred_element_type=jnp.float32)

    result = lax.map(
        translate_block, local_ids.reshape(box_count // stride, stride, lists.shape[1])
    )
    return result.reshape(box_count, window.shape[1], window.shape[2])


def child_shift(shift_child, octants, parents):
    return jnp.einsum(
        "bij,bjn->bin", shift_child[octants], parents, preferred_element_type=jnp.float32
    )


def body(
    parent_local,
    poles_mid,
    poles_fine,
    transfer_mid,
    transfer_fine,
    shift_child,
    lists_mid,
    lists_fine,
    octant_mid,
    octant_fine,
    parent_fine,
):
    space_pos = lax.axis_index("space")
    panels_mid, panels_fine = (
        lax.all_gather(poles_mid, "sub", axis=0, tiled=True),
        lax.all_gather(poles_fine, "sub", axis=0, tiled=True),
    )
    table_mid, table_fine, octs_mid, octs_fine, parent_ids = (
        lists_mid,
        lists_fine,
        octant_mid,
        octant_fine,
        parent_fine,
    )
    mid_rows = panels_mid.shape[0]
    fine_rows = panels_fine.shape[0]
    win_mid = padded(panels_mid, (("space", 0),), mid_rows)
    win_fine = padded(panels_fine, (("space", 0),), fine_rows)
    far_mid = far_field(transfer_mid, win_mid, table_mid, (space_pos - 1) * mid_rows)
    coarse_term = jnp.einsum(
        "bij,jn->bin", shift_child[octs_mid], parent_local[0], preferred_element_type=jnp.float32
    )
    level_mid = (coarse_term + far_mid).astype(jnp.bfloat16)
    far_fine = far_field(transfer_fine, win_fine, table_fine, (space_pos - 1) * fine_rows)
    partition_mid = lax.all_gather(level_mid, "sub", axis=0, tiled=True)
    parents = partition_mid[parent_ids - space_pos * mid_rows]
    level_fine = (child_shift(shift_child, octs_fine, parents) + far_fine).astype(jnp.bfloat16)
    return level_fine


def solution(mesh):
    placed = (
        P("space", None, None),
        P(("space", "sub"), None, None),
        P(("space", "sub"), None, None),
        P(),
        P(),
        P(),
        P(("space", "sub"), None),
        P(("space", "sub"), None),
        P(("space", "sub")),
        P(("space", "sub")),
        P(("space", "sub")),
    )
    return jax.shard_map(
        body, mesh=mesh, in_specs=placed, out_specs=P(("space", "sub"), None, None), check_vma=False
    )
```

profile of v0, /device:TPU:7, one launch (start us, length us, event | category | flops | bytes accessed | tf_op | source)
XLA Modules:
  0.0 296.9 jit_solution(2496037576696327629)
XLA Ops:
  6.5 0.0 copy-start
  6.5 0.0 copy-start.1
  6.5 0.0 all-gather.3.cloned.1.call-start
  6.5 0.7 all-gather.3.cloned.1.call-update
  7.3 51.1 %all_gather.9 = bf16[16,64,128]{2,1,0:T(8,128)(2,1)S(1)} all-gather(bf16[1,64,128]{2,1,0:T(8,128)(2,1)} %param.14), channel_id=1, replica_groups=mesh['space'=32,'sub'=16] {'sub'}, dimensions={0}, use_global_device_ids=true | all-gather | bytes 278528 | tf_op jit(solution)/shard_map/all_gather | solution.py:60
  58.3 2.4 collective-permute-start.1
  60.8 4.9 %collective-permute-start = (bf16[16,64,128]{2,1,0:T(8,128)(2,1)S(1)}, bf16[16,64,128]{2,1,0:T(8,128)(2,1)S(1)}, u32[]{:S(2)}, u32[]{:S(2)}) collective-permute-start(bf16[16,64,128]{2,1,0:T(8,128)(2,1)S(1)} %all_gather.9), channel_id=1, source_target_pairs={{0,16},{16,32},{32,48},{48,64},{64,80},{80,96},{96,112},{112,128},... | collective-permute-start | bytes 786440 | tf_op jit(solution)/shard_map/ppermute | solution.py:14
  65.7 42.6 %all-gather.3.cloned.1.call-done = bf16[128,64,128]{2,1,0:T(8,128)(2,1)} async-done(((bf16[8,64,128]{2,1,0:T(8,128)(2,1)}), bf16[128,64,128]{2,1,0:T(8,128)(2,1)}) %all-gather.3.cloned.1.call-update) | async-done | bytes 2097168 | tf_op jit(solution)/shard_map/all_gather | solution.py:61
  108.4 2.5 collective-permute-start.3
  110.8 4.9 %collective-permute-start.2 = (bf16[128,64,128]{2,1,0:T(8,128)(2,1)}, bf16[128,64,128]{2,1,0:T(8,128)(2,1)}, u32[]{:S(2)}, u32[]{:S(2)}) collective-permute-start(bf16[128,64,128]{2,1,0:T(8,128)(2,1)} %all-gather.3.cloned.1.call-done), channel_id=1, source_target_pairs={{0,16},{16,32},{32,48},{48,64},{64,80},{80,96},{96,112},{112,128},... | collective-permute-start | bytes 6291464 | tf_op jit(solution)/shard_map/ppermute | solution.py:14
  115.8 0.7 compare_select_fusion.6
  116.4 0.7 compare_select_fusion.2
  117.1 0.7 compare_reduce_fusion
  117.8 0.7 compare_select_fusion.5
  118.5 0.7 subtract_select_fusion
  119.2 4.1 %copy.19 = bf16[189,64,64]{0,1,2:T(8,128)(2,1)} copy(bf16[189,64,64]{0,2,1:T(8,128)(2,1)} %param.17) | data formatting | bytes 3096576 | tf_op jit(solution)/shard_map/while | solution.py:33
  123.3 0.0 copy-start.3
  124.0 0.0 copy-done.1
  124.0 5.3 %copy.22 = bf16[189,64,64]{1,2,0:T(8,128)(2,1)} copy(bf16[189,64,64]{0,2,1:T(8,128)(2,1)S(1)} %copy-done.1) | data formatting | bytes 3096576 | tf_op args[3]
  129.3 0.0 copy-done
  129.3 0.6 gather_fusion.1
  129.8 0.0 copy-done.3
  129.9 0.1 fusion.25
  130.0 0.0 collective-permute-done.1
  130.0 0.0 collective-permute-done
  130.0 0.1 pad_maximum_fusion.1
  130.1 2.7 gather_fusion.2
  132.8 4.2 %fusion.21 = bf16[64,128]{1,0:T(8,128)(2,1)S(1)} fusion(f32[64,128]{1,0:T(8,128)S(1)} %fusion.25, bf16[189,64,64]{1,2,0:T(8,128)(2,1)} %copy.22, bf16[189,64,128]{2,1,0:T(8,128)(2,1)} %gather_fusion.2, pred[189]{0:T(512)(128)(4,1)S(1)} %compare_reduce_fusion), kind=kOutput, calls=%fused_computation.23 | convolution fusion | flops 199745536 | bytes 4694205 | tf_op jit(solution)/shard_map/while/body/eval_jaxpr/cij,gcjn->gin/dot_general | solution.py:31
  137.0 58.1 %all-gather = bf16[1024,128]{1,0:T(8,128)(2,1)S(1)} all-gather(bf16[64,128]{1,0:T(8,128)(2,1)S(1)} %fusion.21), channel_id=2, replica_groups=mesh['space'=32,'sub'=16] {'sub'}, dimensions={0}, use_global_device_ids=true | all-gather | bytes 278528 | tf_op jit(solution)/shard_map/all_gather | solution.py:80
  195.0 0.6 gather_fusion.3
  195.6 0.0 copy-start.2
  195.6 0.0 collective-permute-done.3
  195.6 0.0 collective-permute-done.2
  195.6 6.2 %pad_maximum_fusion = bf16[384,64,128]{2,1,0:T(8,128)(2,1)} fusion(bf16[128,64,128]{2,1,0:T(8,128)(2,1)} %collective-permute-done.3, bf16[128,64,128]{2,1,0:T(8,128)(2,1)} %all-gather.3.cloned.1.call-done, bf16[128,64,128]{2,1,0:T(8,128)(2,1)} %collective-permute-done.2), kind=kLoop, calls=%fused_computation.16 | loop fusion | flops 6291456 | bytes 12582912 | tf_op jit(solution)/shard_map/concatenate | solution.py:18
  201.9 0.0 copy-done.2
  201.9 87.3 %while.3 = (s32[]{:T(128)}, f32[2,4,64,128]{3,2,1,0:T(8,128)S(1)}, s32[2,4,189]{2,1,0:T(4,128)S(1)}, bf16[384,64,128]{2,1,0:T(8,128)(2,1)}, bf16[189,64,64]{0,1,2:T(8,128)(2,1)S(1)}, /*index=5*/s32[]{:T(128)}) while((s32[]{:T(128)}, f32[2,4,64,128]{3,2,1,0:T(8,128)S(1)}, s32[2,4,189]{2,1,0:T(4,128)S(1)}, bf16[384,64,128]{2,1,0:T(8,128)(2,1)}, ...), condition=%wide.region_1.2_spmd, body=%wide.region_0.1_spmd.sunk | while | flops 798922176 | bytes 39414268 | solution.py:33
  201.9 0.1 reshape.136
  202.0 22.4 %gather_fusion = bf16[756,64,128]{2,1,0:T(8,128)(2,1)} fusion(bf16[384,64,128]{2,1,0:T(8,128)(2,1)} %get-tuple-element.125, s32[1024]{0:T(1024)S(1)} %pad_clamp_fusion.5), kind=kCustom, calls=%fused_computation.clone.1 | custom fusion | bytes 24775632 | tf_op jit(solution)/shard_map/while/body/eval_jaxpr/gather | solution.py:29
  224.5 21.1 %fusion.37 = f32[2,4,64,128]{3,2,1,0:T(8,128)S(1)} fusion(f32[2,4,64,128]{3,2,1,0:T(8,128)S(1)} %get-tuple-element.117, s32[]{:T(128)S(6)} %copy.35, bf16[189,64,64]{0,1,2:T(8,128)(2,1)S(1)} %get-tuple-element.126, bf16[4,189,64,128]{3,2,1,0:T(8,128)(2,1)} %bitcast.60, pred[4,189]{1,0:T(4,128)(4,1)S(1)} %compare_bitcast_fusion.2), kind=kOutput, calls=%fused_computation.10.clone.1 | convolution fusion | flops 798916608 | bytes 14615556 | tf_op jit(solution)/shard_map/while/body/eval_jaxpr/cij,gcjn->gin/dot_general | solution.py:31
  245.6 0.1 reshape.136
  245.7 22.4 %gather_fusion = bf16[756,64,128]{2,1,0:T(8,128)(2,1)} fusion(bf16[384,64,128]{2,1,0:T(8,128)(2,1)} %get-tuple-element.125, s32[1024]{0:T(1024)S(1)} %pad_clamp_fusion.5), kind=kCustom, calls=%fused_computation.clone.1 | custom fusion | bytes 24775632 | tf_op jit(solution)/shard_map/while/body/eval_jaxpr/gather | solution.py:29
  268.1 21.1 %fusion.37 = f32[2,4,64,128]{3,2,1,0:T(8,128)S(1)} fusion(f32[2,4,64,128]{3,2,1,0:T(8,128)S(1)} %get-tuple-element.117, s32[]{:T(128)S(6)} %copy.35, bf16[189,64,64]{0,1,2:T(8,128)(2,1)S(1)} %get-tuple-element.126, bf16[4,189,64,128]{3,2,1,0:T(8,128)(2,1)} %bitcast.60, pred[4,189]{1,0:T(4,128)(4,1)S(1)} %compare_bitcast_fusion.2), kind=kOutput, calls=%fused_computation.10.clone.1 | convolution fusion | flops 798916608 | bytes 14615556 | tf_op jit(solution)/shard_map/while/body/eval_jaxpr/cij,gcjn->gin/dot_general | solution.py:31
  289.2 0.8 fusion.24
  (11 shorter events, 0.1 us)
Async XLA Ops:
  6.5 122.7 %copy-start = (bf16[8,64,64]{2,1,0:T(8,128)(2,1)S(1)}, bf16[8,64,64]{2,1,0:T(8,128)(2,1)}, u32[]{:S(2)}) copy-start(bf16[8,64,64]{2,1,0:T(8,128)(2,1)} %param.18) | copy-start | bytes 196612
  6.5 117.4 %copy-start.1 = (bf16[189,64,64]{0,2,1:T(8,128)(2,1)S(1)}, bf16[189,64,64]{0,2,1:T(8,128)(2,1)}, u32[]{:S(2)}) copy-start(bf16[189,64,64]{0,2,1:T(8,128)(2,1)} %param.16) | copy-start | bytes 4644868
  6.5 101.8 %all-gather.3.cloned.1.call-start = ((), (), s32[]{:S(2)}) async-start(), calls=%async_computation | async-start | bytes 2228224 | tf_op jit(solution)/shard_map/all_gather | solution.py:61
  58.3 71.6 %collective-permute-start.1 = (bf16[16,64,128]{2,1,0:T(8,128)(2,1)S(1)}, bf16[16,64,128]{2,1,0:T(8,128)(2,1)S(1)}, u32[]{:S(2)}, u32[]{:S(2)}) collective-permute-start(bf16[16,64,128]{2,1,0:T(8,128)(2,1)S(1)} %all_gather.9), channel_id=1, source_target_pairs={{16,0},{32,16},{48,32},{64,48},{80,64},{96,80},{112,96},{128,112},... | collective-permute-start | bytes 786440 | tf_op jit(solution)/shard_map/ppermute | solution.py:17
  60.8 69.2 %collective-permute-start = (bf16[16,64,128]{2,1,0:T(8,128)(2,1)S(1)}, bf16[16,64,128]{2,1,0:T(8,128)(2,1)S(1)}, u32[]{:S(2)}, u32[]{:S(2)}) collective-permute-start(bf16[16,64,128]{2,1,0:T(8,128)(2,1)S(1)} %all_gather.9), channel_id=1, source_target_pairs={{0,16},{16,32},{32,48},{48,64},{64,80},{80,96},{96,112},{112,128},... | collective-permute-start | bytes 786440 | tf_op jit(solution)/shard_map/ppermute | solution.py:14
  108.4 87.3 %collective-permute-start.3 = (bf16[128,64,128]{2,1,0:T(8,128)(2,1)}, bf16[128,64,128]{2,1,0:T(8,128)(2,1)}, u32[]{:S(2)}, u32[]{:S(2)}) collective-permute-start(bf16[128,64,128]{2,1,0:T(8,128)(2,1)} %all-gather.3.cloned.1.call-done), channel_id=1, source_target_pairs={{16,0},{32,16},{48,32},{64,48},{80,64},{96,80},{112,96},{128,112},... | collective-permute-start | bytes 6291464 | tf_op jit(solution)/shard_map/ppermute | solution.py:17
  110.8 84.8 %collective-permute-start.2 = (bf16[128,64,128]{2,1,0:T(8,128)(2,1)}, bf16[128,64,128]{2,1,0:T(8,128)(2,1)}, u32[]{:S(2)}, u32[]{:S(2)}) collective-permute-start(bf16[128,64,128]{2,1,0:T(8,128)(2,1)} %all-gather.3.cloned.1.call-done), channel_id=1, source_target_pairs={{0,16},{16,32},{32,48},{48,64},{64,80},{80,96},{96,112},{112,128},... | collective-permute-start | bytes 6291464 | tf_op jit(solution)/shard_map/ppermute | solution.py:14
  123.3 6.5 %copy-start.3 = (bf16[1,64,128]{2,1,0:T(8,128)(2,1)S(1)}, bf16[1,64,128]{2,1,0:T(8,128)(2,1)}, u32[]{:S(2)}) copy-start(bf16[1,64,128]{2,1,0:T(8,128)(2,1)} %param.13) | copy-start | bytes 49156
  195.6 6.3 %copy-start.2 = (bf16[189,64,64]{0,1,2:T(8,128)(2,1)S(1)}, bf16[189,64,64]{0,1,2:T(8,128)(2,1)}, u32[]{:S(2)}) copy-start(bf16[189,64,64]{0,1,2:T(8,128)(2,1)} %copy.19) | copy-start | bytes 4644868
Sparse Core Ops, SparseCore 0:
  10.7 97.6 all-gather.2
where the time goes:
time: 297 us
  blocking collectives  109 us (37%)
  local copies, waits for them, and re-layouts  58.3 us (20%)
  matrix products  47.3 us (16%)
  waiting for transfers between devices  43.3 us (15%)
  starting transfers between devices  14.8 us (5%)
  between operations  14.2 us (5%)
  other arithmetic  9.82 us (3%)
    all_gather x1, blocking collectives, body(): partition_mid = lax.all_gather(level_mid, 'sub', axis=0, tiled=True)  58.1 us
    all_gather x1, blocking collectives, body(): lax.all_gather(poles_mid, 'sub', axis=0, tiled=True)  51.1 us
    gather x3, local copies, waits for them, and re-layouts, translate_block(): picked = window[jnp.where(present, entries, 0)]  47.6 us
    dot_general x3, matrix products, translate_block(): jnp.einsum('cij,gcjn->gin', operators, picked, preferred_element_type=jnp...  46.3 us
    all_gather x1, waiting for transfers between devices, body(): lax.all_gather(poles_fine, 'sub', axis=0, tiled=True)  42.6 us
    ppermute x2, starting transfers between devices, padded(): lax.ppermute(lax.slice_in_dim(block, block.shape[dim] - width, None, axis...  9.85 us
    concatenate x2, other arithmetic, padded(): block = jnp.concatenate([low, block, high], axis=dim)  6.33 us
  transfers between devices with their start and end apart: 5, of which 1 were waited for; matrix products, arithmetic and copies ran while one was open for 7% of the time, Pallas kernels for 0%

commit v1 on v0

v1 whole, which is shorter than its diff:
```python
import functools

import jax
import jax.numpy as jnp
from jax import lax
from jax.experimental import pallas as pl
from jax.experimental.pallas import tpu as pltpu
from jax.sharding import PartitionSpec as P

MESH = pl.DeviceIdType.MESH
FAR = 189
SHIFT = 192
HALF = 100
FINE_STEPS, FINE_WORDS = 10, 10
MID_STEPS, MID_WORDS = 4, 25
ZERO_FINE, MID_FINE = 384, 385
ZERO_MID, PARENT_MID = 48, 49


def kernel(
    parent_ref,
    mid_ref,
    fine_ref,
    tmid_hbm,
    tfine_hbm,
    shift_hbm,
    lmid_ref,
    lfine_ref,
    omid_ref,
    ofine_ref,
    pfine_ref,
    out_ref,
    ops_fine,
    ops_mid,
    w_fine,
    w_mid,
    stage,
    raw,
    table,
    table_mid,
    ext,
    words,
    steps_fine,
    steps_mid,
    flipped,
    level,
    level_in,
    result,
    result_in,
    sm_even,
    sm_odd,
    sm_mid,
    op_sem,
    sm_sem,
    a2a_send,
    a2a_recv,
    list_send,
    list_recv,
    twin_send,
    twin_recv,
    side_send,
    side_recv,
    level_send,
    level_recv,
    out_send,
    out_recv,
):
    space = lax.axis_index("space")
    sub = lax.axis_index("sub")
    core = sub % 2
    group = sub // 2
    z_hi = group // 4
    y = group % 4
    twin = (space, group * 2 + 1 - core)

    owners = [(1 - z_hi) * 4 + (y + j) % 4 for j in range(4)]
    owners += [z_hi * 4 + (y + j) % 4 for j in range(4)]
    OWN = 4

    def peer(owner):
        return (space, owner * 2 + core)

    def remote(src, dst, send, recv, device):
        return pltpu.make_async_remote_copy(
            src_ref=src, dst_ref=dst, send_sem=send, recv_sem=recv, device_id=device, device_id_type=MESH
        )

    barrier = pltpu.get_barrier_semaphore()
    for j in range(8):
        if j != OWN:
            pl.semaphore_signal(barrier, inc=1, device_id=peer(owners[j]), device_id_type=MESH)
    pl.semaphore_signal(barrier, inc=1, device_id=twin, device_id_type=MESH)

    @pl.when(space > 0)
    def _():
        pl.semaphore_signal(barrier, inc=1, device_id=(space - 1, sub), device_id_type=MESH)

    @pl.when(space < 31)
    def _():
        pl.semaphore_signal(barrier, inc=1, device_id=(space + 1, sub), device_id_type=MESH)

    op_copies = [
        pltpu.make_async_copy(tmid_hbm, ops_mid.at[pl.ds(0, FAR)], op_sem.at[0]),
        pltpu.make_async_copy(shift_hbm, ops_mid.at[pl.ds(SHIFT, 8)], op_sem.at[1]),
        pltpu.make_async_copy(tfine_hbm, ops_fine.at[pl.ds(0, FAR)], op_sem.at[2]),
        pltpu.make_async_copy(shift_hbm, ops_fine.at[pl.ds(SHIFT, 8)], op_sem.at[3]),
    ]
    for c in op_copies:
        c.start()

    low = lax.broadcasted_iota(jnp.int32, (8, 128), 1) < 64
    for i in range(4):
        pair = fine_ref[2 * i : 2 * i + 2].reshape(128, 128).astype(jnp.float32).T
        for g in range(8):
            a = pair[16 * g : 16 * g + 8]
            b = pair[16 * g + 8 : 16 * g + 16]
            first = jnp.where(low, a, pltpu.roll(b, 64, 1))
            second = jnp.where(low, pltpu.roll(a, 64, 1), b)
            stage[g, 16 * i : 16 * i + 16] = jnp.concatenate([first, second], 0).astype(jnp.bfloat16)

    def doubled(panel):
        panel = panel.astype(jnp.float32)
        return jnp.concatenate([panel, panel], 0).T

    box = doubled(mid_ref[0])
    for g in range(8):
        rows = jnp.where(low, box[16 * g : 16 * g + 8], box[16 * g + 8 : 16 * g + 16])
        stage[g, 64:80] = jnp.concatenate([rows, jnp.zeros_like(rows)], 0).astype(jnp.bfloat16)
    flipped[...] = doubled(parent_ref[0])

    ext[0:8, 0:FAR] = lfine_ref[...]
    ext[8:9, 0:FAR] = lmid_ref[...]
    entry = ext[...]
    row = lax.broadcasted_iota(jnp.int32, (16, 256), 0)
    lane = lax.broadcasted_iota(jnp.int32, (16, 256), 1)
    octant = jnp.where(row == 8, omid_ref[0], -1)
    parent = jnp.where(row == 8, PARENT_MID, 0)
    for t in range(8):
        octant = jnp.where(row == t, ofine_ref[t], octant)
        parent = jnp.where(row == t, MID_FINE + jnp.clip(pfine_ref[t] - space * 16, 0, 15), parent)
    nothing = jnp.where(row < 8, ZERO_FINE, ZERO_MID)
    start = jnp.where(row < 8, (space - 1) * 128, (space - 1) * 16)
    last = jnp.where(row < 8, ZERO_FINE, ZERO_MID) - 1
    far = jnp.where(entry >= 0, jnp.clip(entry - start, 0, last), nothing)
    near = jnp.where(lane - SHIFT == octant, parent, nothing)
    rows = jnp.where(lane < FAR, far, near)
    packed = rows[:, :128] + pltpu.roll(rows, 256 - HALF, 1)[:, :128] * 65536
    for j in [OWN]:
        words[owners[j]] = packed

    pl.semaphore_wait(barrier, 8 + (space + 31) // 32 + (62 - space) // 32)

    own = owners[OWN]
    for j in range(8):
        if j != OWN:
            o = owners[j]
            remote(words.at[own], words.at[own], list_send.at[o], list_recv.at[own], peer(o)).start()
            remote(stage.at[o], raw.at[1, core, own], a2a_send.at[o], a2a_recv.at[own], peer(o)).start()
    raw[1, core, own] = stage[own]

    def forward(o):
        piece = raw.at[1, core, o]
        remote(piece, piece, twin_send.at[1, o], twin_recv.at[1, o], twin).start()

        @pl.when(space < 31)
        def _():
            remote(
                piece, raw.at[0, core, o], side_send.at[0, o], side_recv.at[0, o], (space + 1, sub)
            ).start()

        @pl.when(space > 0)
        def _():
            remote(
                piece, raw.at[2, core, o], side_send.at[1, o], side_recv.at[1, o], (space - 1, sub)
            ).start()

    def fill(rel, c, o):
        first = rel * 128 + (o * 2 + c) * 8
        piece = raw[rel, c, o].astype(jnp.float32)
        table[pl.ds(first, 8)] = piece[0:64].reshape(8, 8, 128)
        mid = rel * 16 + o * 2 + c
        table_mid[mid] = piece[64:72]

    forward(own)
    fill(1, core, own)

    for c in op_copies:
        c.wait()
    blank = jnp.zeros((64, 64), jnp.bfloat16)
    for ops, w, steps, count in (
        (ops_mid, w_mid, MID_STEPS, MID_WORDS),
        (ops_fine, w_fine, FINE_STEPS, FINE_WORDS),
    ):
        for c in range(FAR, SHIFT):
            ops[c] = blank

        def lay(m, carry, ops=ops, w=w, count=count):
            for q in range(count):
                for h in range(2):
                    op = ops[m * count + q + HALF * h]
                    at = (2 * q + h) * 128
                    w[m, 0:64, at : at + 128] = jnp.concatenate([op, blank], 1)
                    w[m, 64:128, at : at + 128] = jnp.concatenate([blank, op], 1)
            return carry

        lax.fori_loop(0, steps, lay, 0)

    table[ZERO_FINE] = jnp.zeros((8, 128), jnp.float32)
    table_mid[ZERO_MID] = jnp.zeros((8, 128), jnp.float32)
    at = pl.multiple_of(group * 16, 16)
    table_mid[PARENT_MID] = jnp.where(
        low, flipped[pl.ds(at, 8), :], flipped[pl.ds(at + 8, 8), :]
    )

    def arrive(o):
        piece = raw.at[1, core, o]
        remote(piece, piece, a2a_send.at[o], a2a_recv.at[o], twin).wait_recv()
        forward(o)
        fill(1, core, o)

    def arrive_side(o):
        for side, rel, there in ((0, 0, space > 0), (1, 2, space < 31)):

            @pl.when(there)
            def _(side=side, rel=rel):
                piece = raw.at[rel, core, o]
                remote(piece, piece, side_send.at[side, o], side_recv.at[side, o], twin).wait_recv()
                remote(piece, piece, twin_send.at[rel, o], twin_recv.at[rel, o], twin).start()
                fill(rel, core, o)

    for j in (5, 6, 7):
        arrive(owners[j])
    for j in (4, 5, 6, 7):
        arrive_side(owners[j])

    for j in range(8):
        if j != OWN:
            o = owners[j]
            remote(words.at[o], words.at[o], list_send.at[o], list_recv.at[o], twin).wait_recv()
    lists = [words[o] for o in owners]
    flat = jnp.concatenate(
        [v[0:8] for v in lists] + [v[8:9] for v in lists] + [jnp.zeros((56, 128), jnp.int32)], 0
    ).T
    for tile in range(2):
        part = pltpu.roll(flat, 128 - 32 * tile, 1) if tile else flat
        for m in range(FINE_STEPS):
            steps_fine[tile, m, 0:FINE_WORDS] = part[m * FINE_WORDS : (m + 1) * FINE_WORDS]
    part = pltpu.roll(flat, 64, 1)
    for m in range(MID_STEPS):
        steps_mid[m, 0:MID_WORDS] = part[m * MID_WORDS : (m + 1) * MID_WORDS]
    mid_lists = pltpu.make_async_copy(steps_mid, sm_mid, sm_sem.at[2])
    mid_lists.start()

    for j in range(4):
        arrive(owners[j])
    for j in range(4):
        arrive_side(owners[j])
    for j in (4, 5, 6, 7, 0, 1, 2, 3):
        o = owners[j]
        for rel, there in ((1, None), (0, space > 0), (2, space < 31)):

            def take(rel=rel, o=o):
                piece = raw.at[rel, 1 - core, o]
                remote(piece, piece, twin_send.at[rel, o], twin_recv.at[rel, o], twin).wait_recv()
                fill(rel, 1 - core, o)

            if there is None:
                take()
            else:
                pl.when(there)(take)

    def product(source, word, targets, count, weights, acc):
        columns = []
        for q in range(count):
            pair = [word(q, t) for t in range(targets)]
            for row in ([v & 0xFFFF for v in pair], [v >> 16 for v in pair]):
                picked = [source[r] for r in row]
                columns.append(jnp.concatenate(picked, 0).astype(jnp.bfloat16))
        return acc + lax.dot_general(
            jnp.concatenate(columns, 1),
            weights,
            (((1,), (1,)), ((), ())),
            preferred_element_type=jnp.float32,
        )

    mid_lists.wait()
    acc = jnp.zeros((64, 128), jnp.float32)
    for m in range(MID_STEPS):
        acc = product(table_mid, lambda q, t, m=m: sm_mid[m, q, t], 8, MID_WORDS, w_mid[m], acc)
    level[...] = acc.astype(jnp.bfloat16)
    to_twin = remote(level, level_in, level_send.at[0], level_recv.at[0], twin)
    to_twin.start()

    def keep(rows, c):
        rows = rows.astype(jnp.float32)
        for j in range(8):
            table[MID_FINE + owners[j] * 2 + c] = rows[8 * j : 8 * j + 8]

    keep(level[...], core)

    for tile in range(2):

        def load(m, buf, k, tile=tile):
            return pltpu.make_async_copy(steps_fine.at[tile, m], buf, sm_sem.at[k])

        load(0, sm_even, 0).start()

        def body(h, acc, tile=tile, load=load):
            if tile == 0:

                @pl.when(h == FINE_STEPS // 2 - 1)
                def _():
                    to_twin.wait_recv()
                    keep(level_in[...], 1 - core)

            load(2 * h, sm_even, 0).wait()
            load(2 * h + 1, sm_odd, 1).start()
            acc = product(
                table, lambda q, t: sm_even[q, t], 32, FINE_WORDS, w_fine[2 * h], acc
            )
            load(2 * h + 1, sm_odd, 1).wait()

            @pl.when(h < FINE_STEPS // 2 - 1)
            def _():
                load(2 * h + 2, sm_even, 0).start()

            return product(
                table, lambda q, t: sm_odd[q, t], 32, FINE_WORDS, w_fine[2 * h + 1], acc
            )

        acc = lax.fori_loop(0, FINE_STEPS // 2, body, jnp.zeros((256, 128), jnp.float32))
        result[tile] = acc.astype(jnp.bfloat16).reshape(4, 64, 128)
        for i in range(4):
            j = 4 * tile + i
            if j != OWN:
                remote(
                    result.at[tile, i], result_in.at[own], out_send.at[j], out_recv.at[own], peer(owners[j])
                ).start()
    result_in[own] = result[1, 0]

    for j in (0, 1, 2, 3, 5, 6, 7):
        o = owners[j]
        remote(result.at[0, 0], result_in.at[o], out_send.at[j], out_recv.at[o], twin).wait_recv()
    for i in range(4):
        rows = []
        for g in range(8):
            both = result_in[g, 16 * i : 16 * i + 16].astype(jnp.float32)
            a, b = both[0:8], both[8:16]
            rows.append(jnp.where(low, a, pltpu.roll(b, 64, 1)))
            rows.append(jnp.where(low, pltpu.roll(a, 64, 1), b))
        out_ref[2 * i : 2 * i + 2] = (
            jnp.concatenate(rows, 0).T.astype(jnp.bfloat16).reshape(2, 64, 128)
        )

    to_twin.wait_send()
    for j in range(8):
        o = owners[j]
        piece = raw.at[1, core, o]
        if j != OWN:
            remote(words.at[o], words.at[o], list_send.at[o], list_recv.at[o], twin).wait_send()
            remote(piece, piece, a2a_send.at[o], a2a_recv.at[o], twin).wait_send()
            remote(result.at[0, 0], result_in.at[o], out_send.at[j], out_recv.at[o], twin).wait_send()
        remote(piece, piece, twin_send.at[1, o], twin_recv.at[1, o], twin).wait_send()
        for side, rel, there, back in ((0, 0, space < 31, space > 0), (1, 2, space > 0, space < 31)):

            @pl.when(there)
            def _(side=side, o=o, piece=piece):
                remote(piece, piece, side_send.at[side, o], side_recv.at[side, o], twin).wait_send()

            @pl.when(back)
            def _(rel=rel, o=o, piece=piece):
                remote(piece, piece, twin_send.at[rel, o], twin_recv.at[rel, o], twin).wait_send()


def body(*args):
    vmem = pl.BlockSpec(memory_space=pltpu.VMEM)
    smem = pl.BlockSpec(memory_space=pltpu.SMEM)
    hbm = pl.BlockSpec(memory_space=pl.ANY)
    bf16, f32, i32 = jnp.bfloat16, jnp.float32, jnp.int32
    dma = pltpu.SemaphoreType.DMA
    return pl.pallas_call(
        kernel,
        out_shape=jax.ShapeDtypeStruct((8, 64, 128), bf16),
        in_specs=[vmem, vmem, vmem, hbm, hbm, hbm, vmem, vmem, smem, smem, smem],
        out_specs=vmem,
        scratch_shapes=[
            pltpu.VMEM((200, 64, 64), bf16),
            pltpu.VMEM((200, 64, 64), bf16),
            pltpu.VMEM((FINE_STEPS, 128, FINE_WORDS * 256), bf16),
            pltpu.VMEM((MID_STEPS, 128, MID_WORDS * 256), bf16),
            pltpu.VMEM((8, 80, 128), bf16),
            pltpu.VMEM((3, 2, 8, 80, 128), bf16),
            pltpu.VMEM((MID_FINE + 16, 8, 128), f32),
            pltpu.VMEM((PARENT_MID + 1, 8, 128), f32),
            pltpu.VMEM((16, 256), i32),
            pltpu.VMEM((8, 16, 128), i32),
            pltpu.VMEM((2, FINE_STEPS, 16, 128), i32),
            pltpu.VMEM((MID_STEPS, 32, 128), i32),
            pltpu.VMEM((128, 128), f32),
            pltpu.VMEM((64, 128), bf16),
            pltpu.VMEM((64, 128), bf16),
            pltpu.VMEM((2, 4, 64, 128), bf16),
            pltpu.VMEM((8, 64, 128), bf16),
            pltpu.SMEM((16, 128), i32),
            pltpu.SMEM((16, 128), i32),
            pltpu.SMEM((MID_STEPS, 32, 128), i32),
            dma((4,)),
            dma((3,)),
            dma((8,)),
            dma((8,)),
            dma((8,)),
            dma((8,)),
            dma((3, 8)),
            dma((3, 8)),
            dma((2, 8)),
            dma((2, 8)),
            dma((1,)),
            dma((1,)),
            dma((8,)),
            dma((8,)),
        ],
        compiler_params=pltpu.CompilerParams(
            collective_id=0, has_side_effects=True, vmem_limit_bytes=48 * 2**20
        ),
    )(*args)


def solution(mesh):
    placed = (
        P("space", None, None),
        P(("space", "sub"), None, None),
        P(("space", "sub"), None, None),
        P(),
        P(),
        P(),
        P(("space", "sub"), None),
        P(("space", "sub"), None),
        P(("space", "sub")),
        P(("space", "sub")),
        P(("space", "sub")),
    )
    return jax.shard_map(
        body, mesh=mesh, in_specs=placed, out_specs=P(("space", "sub"), None, None), check_vma=False
    )
```

time: 297 us -> 82.1 us (0.28)
  blocking collectives: 109 us -> 0 us
  Pallas kernels: 0 us -> 70 us
  local copies, waits for them, and re-layouts: 58.3 us -> 10.8 us
  matrix products: 47.3 us -> 0 us
  waiting for transfers between devices: 43.3 us -> 0 us
  starting transfers between devices: 14.8 us -> 0 us
  between operations: 14.2 us -> 0.78 us
  other arithmetic: 9.82 us -> 0 us
    all_gather x2 -> x0, blocking collectives: 109 us -> none  [the longest x1 58.1 us: body(): partition_mid = lax.all_gather(level_mid, 'sub', axis=0, tiled=True)]
    pallas_call x0 -> x1, Pallas kernels: none -> 70 us  [body(): pl.pallas_call(kernel, out_shape=jax.ShapeDtypeStruct((8, 64, 128), bf16)...]
    gather x5 -> x0, local copies, waits for them, and re-layouts: 48.7 us -> none  [the longest x3 47.6 us: translate_block(): picked = window[jnp.where(present, entries, 0)]]
    dot_general x5 -> x0, matrix products: 47.3 us -> none  [the longest x3 46.3 us: translate_block(): jnp.einsum('cij,gcjn->gin', operators, picked, preferred_element_type=jnp...]
    all_gather x1 -> x0, waiting for transfers between devices: 42.6 us -> none  [body(): lax.all_gather(poles_fine, 'sub', axis=0, tiled=True)]
    ppermute x4 -> x0, starting transfers between devices: 14.8 us -> none  [the longest x2 9.85 us: padded(): lax.ppermute(lax.slice_in_dim(block, block.shape[dim] - width, None, axis...]
    concatenate x2 -> x0, other arithmetic: 6.33 us -> none  [padded(): block = jnp.concatenate([low, block, high], axis=dim)]
    unnamed x9 -> x19, local copies, waits for them, and re-layouts: 5.3 us -> 10.8 us
  transfers between devices with their start and end apart: 5 -> 0, of which waited for: 1 -> 0; matrix products, arithmetic and copies ran while one was open for 7% -> 0% of each run, Pallas kernels for 0% -> 0%
where the time goes in v1:
time: 82.1 us; the launch traced here: 81.5 us
  Pallas kernels  70 us (85%)
  local copies, waits for them, and re-layouts  10.8 us (13%)
    pallas_call x1, Pallas kernels, body(): pl.pallas_call(kernel, out_shape=jax.ShapeDtypeStruct((8, 64, 128), bf16)...  70 us
    unnamed x19, local copies, waits for them, and re-layouts  10.8 us

profile of v1, /device:TPU:7, one launch (start us, length us, event | category | flops | bytes accessed | tf_op | source)
XLA Modules:
  0.0 81.5 jit_solution(10819416899905568526)
XLA Ops:
  0.7 4.5 %copy.12.tmid_hbm = bf16[189,64,64]{2,1,0:T(8,128)(2,1)S(1)} copy(bf16[189,64,64]{0,2,1:T(8,128)(2,1)} %param.14) | data formatting | bytes 3096576 | tf_op args[3]
  5.2 0.0 copy-start
  5.2 0.0 copy-start.1
  5.2 0.0 copy-start.2
  5.2 0.0 copy-start.3
  5.2 0.0 copy-start.4
  5.2 0.0 copy-start.5
  5.2 0.0 copy-start.6
  5.2 0.0 copy-start.7
  5.3 5.6 %copy.13.tfine_hbm = bf16[189,64,64]{2,1,0:T(8,128)(2,1)} copy(bf16[189,64,64]{0,2,1:T(8,128)(2,1)} %param.15) | data formatting | bytes 3096576 | tf_op args[4]
  10.8 0.0 copy-done
  10.8 0.0 copy-done.1
  10.8 0.0 copy-done.2
  10.8 0.0 copy-done.3
  10.8 0.0 copy-done.4
  10.8 0.0 copy-done.5
  10.9 0.0 copy-done.6
  10.9 0.0 copy-done.7
  10.9 70.0 %shard_map.109 = bf16[8,64,128]{2,1,0:T(8,128)(2,1)S(1)} custom-call(bf16[1,64,128]{2,1,0:T(8,128)(2,1)S(1)} %copy-done.2, bf16[1,64,128]{2,1,0:T(8,128)(2,1)S(1)} %copy-done.3, bf16[8,64,128]{2,1,0:T(8,128)(2,1)S(1)} %copy-done, bf16[189,64,64]{2,1,0:T(8,128)(2,1)S(1)} %copy.12.tmid_hbm, bf16[189,64,64]{2,1,0:T(8,128)(2,1)} %copy.13.tfine_hbm, ...), custom_call_target="tpu_custom_call" | custom-call | tf_op jit(solution)/shard_map/pallas_call | solution.py:381
  80.8 0.7 copy.16
Async XLA Ops:
  5.2 5.7 %copy-start = (bf16[8,64,128]{2,1,0:T(8,128)(2,1)S(1)}, bf16[8,64,128]{2,1,0:T(8,128)(2,1)}, u32[]{:S(2)}) copy-start(bf16[8,64,128]{2,1,0:T(8,128)(2,1)} %fine_ref.1) | copy-start | bytes 393220
  5.2 5.6 %copy-start.1 = (bf16[8,64,64]{2,1,0:T(8,128)(2,1)S(1)}, bf16[8,64,64]{2,1,0:T(8,128)(2,1)}, u32[]{:S(2)}) copy-start(bf16[8,64,64]{2,1,0:T(8,128)(2,1)} %shift_hbm.1) | copy-start | bytes 196612
  5.2 5.6 %copy-start.2 = (bf16[1,64,128]{2,1,0:T(8,128)(2,1)S(1)}, bf16[1,64,128]{2,1,0:T(8,128)(2,1)}, u32[]{:S(2)}) copy-start(bf16[1,64,128]{2,1,0:T(8,128)(2,1)} %parent_ref.1) | copy-start | bytes 49156
  5.2 5.6 %copy-start.3 = (bf16[1,64,128]{2,1,0:T(8,128)(2,1)S(1)}, bf16[1,64,128]{2,1,0:T(8,128)(2,1)}, u32[]{:S(2)}) copy-start(bf16[1,64,128]{2,1,0:T(8,128)(2,1)} %mid_ref.1) | copy-start | bytes 49156
  5.2 5.6 %copy-start.4 = (s32[8,189]{1,0:T(8,128)S(1)}, s32[8,189]{1,0:T(8,128)}, u32[]{:S(2)}) copy-start(s32[8,189]{1,0:T(8,128)} %lfine_ref.1) | copy-start | bytes 18148
  5.2 5.6 %copy-start.5 = (s32[1,189]{1,0:T(1,128)S(1)}, s32[1,189]{1,0:T(1,128)}, u32[]{:S(2)}) copy-start(s32[1,189]{1,0:T(1,128)} %lmid_ref.1) | copy-start | bytes 2272
  5.2 5.6 %copy-start.6 = (s32[8]{0:T(128)S(1)}, s32[8]{0:T(128)}, u32[]{:S(2)}) copy-start(s32[8]{0:T(128)} %ofine_ref.1) | copy-start | bytes 100
  5.2 5.6 %copy-start.7 = (s32[8]{0:T(128)S(1)}, s32[8]{0:T(128)}, u32[]{:S(2)}) copy-start(s32[8]{0:T(128)} %pfine_ref.1) | copy-start | bytes 100

commit v2 on v1

--- a/solution.py
+++ b/solution.py
@@ -11,27 +11,38 @@
 FAR = 189
 SHIFT = 192
 HALF = 100
-FINE_STEPS, FINE_WORDS = 10, 10
-MID_STEPS, MID_WORDS = 4, 25
+STEPS, WORDS = 4, 25
+SPARE = 13
 ZERO_FINE, MID_FINE = 384, 385
 ZERO_MID, PARENT_MID = 48, 49
 
 
 def kernel(
+    parent_hbm,
+    mid_hbm,
+    fine_hbm,
+    tmid_hbm,
+    tfine_hbm,
+    shift_hbm,
+    lmid_hbm,
+    lfine_hbm,
+    omid_hbm,
+    ofine_hbm,
+    pfine_hbm,
+    out_ref,
     parent_ref,
     mid_ref,
     fine_ref,
-    tmid_hbm,
-    tfine_hbm,
-    shift_hbm,
+    shift_ref,
     lmid_ref,
     lfine_ref,
     omid_ref,
     ofine_ref,
     pfine_ref,
-    out_ref,
     ops_fine,
     ops_mid,
+    turned,
+    shift_wide,
     w_fine,
     w_mid,
     stage,
@@ -43,12 +54,12 @@
     steps_fine,
     steps_mid,
     flipped,
+    unpermuted,
     level,
     level_in,
     result,
     result_in,
-    sm_even,
-    sm_odd,
+    sm_fine,
     sm_mid,
     op_sem,
     sm_sem,
@@ -99,14 +110,24 @@
     def _():
         pl.semaphore_signal(barrier, inc=1, device_id=(space + 1, sub), device_id_type=MESH)
 
-    op_copies = [
-        pltpu.make_async_copy(tmid_hbm, ops_mid.at[pl.ds(0, FAR)], op_sem.at[0]),
-        pltpu.make_async_copy(shift_hbm, ops_mid.at[pl.ds(SHIFT, 8)], op_sem.at[1]),
-        pltpu.make_async_copy(tfine_hbm, ops_fine.at[pl.ds(0, FAR)], op_sem.at[2]),
-        pltpu.make_async_copy(shift_hbm, ops_fine.at[pl.ds(SHIFT, 8)], op_sem.at[3]),
-    ]
-    for c in op_copies:
+    copies = (
+        (fine_hbm, fine_ref),
+        (mid_hbm, mid_ref),
+        (lfine_hbm, lfine_ref),
+        (lmid_hbm, lmid_ref),
+        (omid_hbm, omid_ref),
+        (ofine_hbm, ofine_ref),
+        (pfine_hbm, pfine_ref),
+        (parent_hbm, parent_ref),
+        (shift_hbm, shift_ref),
+        (tmid_hbm, ops_mid),
+        (tfine_hbm, ops_fine),
+    )
+    copies = [pltpu.make_async_copy(a, b, op_sem.at[i]) for i, (a, b) in enumerate(copies)]
+    for c in copies:
         c.start()
+    for c in copies[:8]:
+        c.wait()
 
     low = lax.broadcasted_iota(jnp.int32, (8, 128), 1) < 64
     for i in range(4):
@@ -145,8 +166,15 @@
     near = jnp.where(lane - SHIFT == octant, parent, nothing)
     rows = jnp.where(lane < FAR, far, near)
     packed = rows[:, :128] + pltpu.roll(rows, 256 - HALF, 1)[:, :128] * 65536
-    for j in [OWN]:
-        words[owners[j]] = packed
+    fine_words = packed[0:8]
+    mid_words = jnp.broadcast_to(packed[8:9], (8, 128))
+    row8 = lax.broadcasted_iota(jnp.int32, (8, 128), 0)
+    lane8 = lax.broadcasted_iota(jnp.int32, (8, 128), 1)
+    spare = (lane8 >= HALF) & (lane8 < HALF + SPARE)
+    for r in range(8):
+        moved = pltpu.roll(mid_words, (HALF - SPARE * r) % 128, 1)
+        fine_words = jnp.where(spare & (row8 == r), moved, fine_words)
+    words[owners[OWN]] = fine_words
 
     pl.semaphore_wait(barrier, 8 + (space + 31) // 32 + (62 - space) // 32)
 
@@ -184,26 +212,45 @@
     forward(own)
     fill(1, core, own)
 
-    for c in op_copies:
-        c.wait()
-    blank = jnp.zeros((64, 64), jnp.bfloat16)
-    for ops, w, steps, count in (
-        (ops_mid, w_mid, MID_STEPS, MID_WORDS),
-        (ops_fine, w_fine, FINE_STEPS, FINE_WORDS),
-    ):
+    copies[8].wait()
+    shift_wide[...] = shift_ref[...].astype(jnp.float32).reshape(512, 64)
+    low32 = lax.broadcasted_iota(jnp.int32, (32, 128), 1) < 64
+
+    def operators(ops, w):
+        def turn(p, carry):
+            both = ops[pl.ds(2 * p, 2)].reshape(128, FAR).astype(jnp.float32)
+            at = pl.multiple_of(p * 200, 8)
+            turned[pl.ds(at, 128), :] = both[:, 0:128].T
+            turned[pl.ds(at + 128, FAR - 128), :] = both[:, 128:FAR].T
+            return carry
+
+        lax.fori_loop(0, 32, turn, 0)
         for c in range(FAR, SHIFT):
-            ops[c] = blank
-
-        def lay(m, carry, ops=ops, w=w, count=count):
-            for q in range(count):
+            turned[pl.ds(c, 32, 200), :] = jnp.zeros((32, 128), jnp.float32)
+        for o in range(8):
+            even = shift_wide[pl.ds(64 * o, 32, 2), :]
+            odd = shift_wide[pl.ds(64 * o + 1, 32, 2), :]
+            turned[pl.ds(SHIFT + o, 32, 200), :] = jnp.concatenate([even, odd], 1)
+
+        def lay(m, carry):
+            for q in range(WORDS):
                 for h in range(2):
-                    op = ops[m * count + q + HALF * h]
+                    op = turned[pl.ds(m * WORDS + q + HALF * h, 32, 200), :]
+                    swapped = pltpu.roll(op, 64, 1)
+                    parts = [
+                        jnp.where(low32, op, 0.0),
+                        jnp.where(low32, swapped, 0.0),
+                        jnp.where(low32, 0.0, swapped),
+                        jnp.where(low32, 0.0, op),
+                    ]
                     at = (2 * q + h) * 128
-                    w[m, 0:64, at : at + 128] = jnp.concatenate([op, blank], 1)
-                    w[m, 64:128, at : at + 128] = jnp.concatenate([blank, op], 1)
+                    w[m, :, at : at + 128] = jnp.concatenate(parts, 0).astype(jnp.bfloat16)
             return carry
 
-        lax.fori_loop(0, steps, lay, 0)
+        lax.fori_loop(0, STEPS, lay, 0)
+
+    copies[9].wait()
+    operators(ops_mid, w_mid)
 
     table[ZERO_FINE] = jnp.zeros((8, 128), jnp.float32)
     table_mid[ZERO_MID] = jnp.zeros((8, 128), jnp.float32)
@@ -232,23 +279,39 @@
         arrive(owners[j])
     for j in (4, 5, 6, 7):
         arrive_side(owners[j])
+    copies[10].wait()
+    operators(ops_fine, w_fine)
 
     for j in range(8):
         if j != OWN:
             o = owners[j]
             remote(words.at[o], words.at[o], list_send.at[o], list_recv.at[o], twin).wait_recv()
-    lists = [words[o] for o in owners]
-    flat = jnp.concatenate(
-        [v[0:8] for v in lists] + [v[8:9] for v in lists] + [jnp.zeros((56, 128), jnp.int32)], 0
-    ).T
+    flat = jnp.concatenate([words[o] for o in owners] + [jnp.zeros((64, 128), jnp.int32)], 0).T
+    lane13 = lax.broadcasted_iota(jnp.int32, (SPARE, 128), 1)
+    halves = (flat & 0xFFFF, flat >> 16)
     for tile in range(2):
-        part = pltpu.roll(flat, 128 - 32 * tile, 1) if tile else flat
-        for m in range(FINE_STEPS):
-            steps_fine[tile, m, 0:FINE_WORDS] = part[m * FINE_WORDS : (m + 1) * FINE_WORDS]
-    part = pltpu.roll(flat, 64, 1)
-    for m in range(MID_STEPS):
-        steps_mid[m, 0:MID_WORDS] = part[m * MID_WORDS : (m + 1) * MID_WORDS]
-    mid_lists = pltpu.make_async_copy(steps_mid, sm_mid, sm_sem.at[2])
+        for m in range(STEPS):
+            rows = [v[m * WORDS : (m + 1) * WORDS] for v in halves]
+            rows = jnp.concatenate(rows + [jnp.zeros((2, 128), jnp.int32)], 0)
+            block = rows[0:SPARE]
+            if tile:
+                block = pltpu.roll(block, 128 - 32, 1)
+            for k in range(1, 4):
+                more = rows[SPARE * k : SPARE * (k + 1)]
+                shift = (32 * k - 32 * tile) % 128
+                if shift:
+                    more = pltpu.roll(more, shift, 1)
+                block = jnp.where(lane13 // 32 == k, more, block)
+            steps_fine[tile, m, 0:SPARE] = block
+    for h, part in enumerate(halves):
+        steps_mid[SPARE * h : SPARE * (h + 1)] = part[HALF : HALF + SPARE]
+
+    def load(tile, m):
+        return pltpu.make_async_copy(steps_fine.at[tile, m], sm_fine.at[m], sm_sem.at[m])
+
+    for m in range(STEPS):
+        load(0, m).start()
+    mid_lists = pltpu.make_async_copy(steps_mid, sm_mid, sm_sem.at[STEPS])
     mid_lists.start()
 
     for j in range(4):
@@ -269,12 +332,11 @@
             else:
                 pl.when(there)(take)
 
-    def product(source, word, targets, count, weights, acc):
+    def product(source, place, targets, weights, acc):
         columns = []
-        for q in range(count):
-            pair = [word(q, t) for t in range(targets)]
-            for row in ([v & 0xFFFF for v in pair], [v >> 16 for v in pair]):
-                picked = [source[r] for r in row]
+        for q in range(WORDS):
+            for h in range(2):
+                picked = [source[place(q, h, t)] for t in range(targets)]
                 columns.append(jnp.concatenate(picked, 0).astype(jnp.bfloat16))
         return acc + lax.dot_general(
             jnp.concatenate(columns, 1),
@@ -285,8 +347,21 @@
 
     mid_lists.wait()
     acc = jnp.zeros((64, 128), jnp.float32)
-    for m in range(MID_STEPS):
-        acc = product(table_mid, lambda q, t, m=m: sm_mid[m, q, t], 8, MID_WORDS, w_mid[m], acc)
+    for m in range(STEPS):
+
+        def place(q, h, t, m=m):
+            word = m * WORDS + q
+            return sm_mid[SPARE * h + word % SPARE, 8 * t + word // SPARE]
+
+        acc = product(table_mid, place, 8, w_mid[m], acc)
+
+    def in_order(panel, at):
+        for half in range(4):
+            first = at + 64 * (half // 2) + half % 2
+            unpermuted[pl.ds(first, 32, 2), :] = panel[32 * half : 32 * half + 32]
+        return unpermuted[at : at + 128]
+
+    acc = in_order(jnp.concatenate([acc, jnp.zeros_like(acc)], 0).T, 0).T[0:64]
     level[...] = acc.astype(jnp.bfloat16)
     to_twin = remote(level, level_in, level_send.at[0], level_recv.at[0], twin)
     to_twin.start()
@@ -298,44 +373,43 @@
 
     keep(level[...], core)
 
-    for tile in range(2):
-
-        def load(m, buf, k, tile=tile):
-            return pltpu.make_async_copy(steps_fine.at[tile, m], buf, sm_sem.at[k])
-
-        load(0, sm_even, 0).start()
-
-        def body(h, acc, tile=tile, load=load):
-            if tile == 0:
-
-                @pl.when(h == FINE_STEPS // 2 - 1)
+    def targets_of(tile, carry):
+        acc = jnp.zeros((256, 128), jnp.float32)
+        for m in range(STEPS):
+            if m == STEPS - 1:
+
+                @pl.when(tile == 0)
                 def _():
                     to_twin.wait_recv()
                     keep(level_in[...], 1 - core)
 
-            load(2 * h, sm_even, 0).wait()
-            load(2 * h + 1, sm_odd, 1).start()
-            acc = product(
-                table, lambda q, t: sm_even[q, t], 32, FINE_WORDS, w_fine[2 * h], acc
-            )
-            load(2 * h + 1, sm_odd, 1).wait()
-
-            @pl.when(h < FINE_STEPS // 2 - 1)
-            def _():
-                load(2 * h + 2, sm_even, 0).start()
-
-            return product(
-                table, lambda q, t: sm_odd[q, t], 32, FINE_WORDS, w_fine[2 * h + 1], acc
-            )
-
-        acc = lax.fori_loop(0, FINE_STEPS // 2, body, jnp.zeros((256, 128), jnp.float32))
+            def place(q, h, t, m=m):
+                at = WORDS * h + q
+                return sm_fine[m, at % SPARE, 32 * (at // SPARE) + t]
+
+            load(tile, m).wait()
+            acc = product(table, place, 32, w_fine[m], acc)
+
+            @pl.when(tile == 0)
+            def _(m=m):
+                load(1, m).start()
+
         result[tile] = acc.astype(jnp.bfloat16).reshape(4, 64, 128)
         for i in range(4):
-            j = 4 * tile + i
-            if j != OWN:
+            o = ((z_hi + 1 + tile) % 2) * 4 + (y + i) % 4
+
+            def send(i=i, o=o):
                 remote(
-                    result.at[tile, i], result_in.at[own], out_send.at[j], out_recv.at[own], peer(owners[j])
+                    result.at[tile, i], result_in.at[own], out_send.at[4 * tile + i], out_recv.at[own], peer(o)
                 ).start()
+
+            if i == 0:
+                pl.when(tile == 0)(send)
+            else:
+                send()
+        return carry
+
+    lax.fori_loop(0, 2, targets_of, 0)
     result_in[own] = result[1, 0]
 
     for j in (0, 1, 2, 3, 5, 6, 7):
@@ -348,9 +422,8 @@
             a, b = both[0:8], both[8:16]
             rows.append(jnp.where(low, a, pltpu.roll(b, 64, 1)))
             rows.append(jnp.where(low, pltpu.roll(a, 64, 1), b))
-        out_ref[2 * i : 2 * i + 2] = (
-            jnp.concatenate(rows, 0).T.astype(jnp.bfloat16).reshape(2, 64, 128)
-        )
+        panel = in_order(jnp.concatenate(rows, 0).T, 128 * i)
+        out_ref[2 * i : 2 * i + 2] = panel.astype(jnp.bfloat16).reshape(2, 64, 128)
 
     to_twin.wait_send()
     for j in range(8):
@@ -372,40 +445,50 @@
                 remote(piece, piece, twin_send.at[rel, o], twin_recv.at[rel, o], twin).wait_send()
 
 
-def body(*args):
+def body(parent, mid, fine, tmid, tfine, *rest):
     vmem = pl.BlockSpec(memory_space=pltpu.VMEM)
-    smem = pl.BlockSpec(memory_space=pltpu.SMEM)
     hbm = pl.BlockSpec(memory_space=pl.ANY)
     bf16, f32, i32 = jnp.bfloat16, jnp.float32, jnp.int32
     dma = pltpu.SemaphoreType.DMA
     return pl.pallas_call(
         kernel,
         out_shape=jax.ShapeDtypeStruct((8, 64, 128), bf16),
-        in_specs=[vmem, vmem, vmem, hbm, hbm, hbm, vmem, vmem, smem, smem, smem],
+        in_specs=[hbm] * 11,
         out_specs=vmem,
         scratch_shapes=[
-            pltpu.VMEM((200, 64, 64), bf16),
-            pltpu.VMEM((200, 64, 64), bf16),
-            pltpu.VMEM((FINE_STEPS, 128, FINE_WORDS * 256), bf16),
-            pltpu.VMEM((MID_STEPS, 128, MID_WORDS * 256), bf16),
+            pltpu.VMEM((1, 64, 128), bf16),
+            pltpu.VMEM((1, 64, 128), bf16),
+            pltpu.VMEM((8, 64, 128), bf16),
+            pltpu.VMEM((8, 64, 64), bf16),
+            pltpu.VMEM((1, FAR), i32),
+            pltpu.VMEM((8, FAR), i32),
+            pltpu.SMEM((1,), i32),
+            pltpu.SMEM((8,), i32),
+            pltpu.SMEM((8,), i32),
+            pltpu.VMEM((64, 64, FAR), bf16),
+            pltpu.VMEM((64, 64, FAR), bf16),
+            pltpu.VMEM((32 * 200, 128), f32),
+            pltpu.VMEM((512, 64), f32),
+            pltpu.VMEM((STEPS, 128, WORDS * 256), bf16),
+            pltpu.VMEM((STEPS, 128, WORDS * 256), bf16),
             pltpu.VMEM((8, 80, 128), bf16),
             pltpu.VMEM((3, 2, 8, 80, 128), bf16),
             pltpu.VMEM((MID_FINE + 16, 8, 128), f32),
             pltpu.VMEM((PARENT_MID + 1, 8, 128), f32),
             pltpu.VMEM((16, 256), i32),
-            pltpu.VMEM((8, 16, 128), i32),
-            pltpu.VMEM((2, FINE_STEPS, 16, 128), i32),
-            pltpu.VMEM((MID_STEPS, 32, 128), i32),
+            pltpu.VMEM((8, 8, 128), i32),
+            pltpu.VMEM((2, STEPS, 16, 128), i32),
+            pltpu.VMEM((32, 128), i32),
             pltpu.VMEM((128, 128), f32),
+            pltpu.VMEM((512, 128), f32),
             pltpu.VMEM((64, 128), bf16),
             pltpu.VMEM((64, 128), bf16),
             pltpu.VMEM((2, 4, 64, 128), bf16),
             pltpu.VMEM((8, 64, 128), bf16),
-            pltpu.SMEM((16, 128), i32),
-            pltpu.SMEM((16, 128), i32),
-            pltpu.SMEM((MID_STEPS, 32, 128), i32),
-            dma((4,)),
-            dma((3,)),
+            pltpu.SMEM((STEPS, 16, 128), i32),
+            pltpu.SMEM((32, 128), i32),
+            dma((11,)),
+            dma((STEPS + 1,)),
             dma((8,)),
             dma((8,)),
             dma((8,)),
@@ -420,9 +503,9 @@
             dma((8,)),
         ],
         compiler_params=pltpu.CompilerParams(
-            collective_id=0, has_side_effects=True, vmem_limit_bytes=48 * 2**20
+            collective_id=0, has_side_effects=True, vmem_limit_bytes=63 * 2**20
         ),
-    )(*args)
+    )(parent, mid, fine, tmid.transpose(1, 2, 0), tfine.transpose(1, 2, 0), *rest)
 
 
 def solution(mesh):

time: 82.1 us -> 66.2 us (0.81)
  local copies, waits for them, and re-layouts: 10.8 us -> 1.57 us
  Pallas kernels: 70 us -> 63 us
    unnamed x19 -> x1, local copies, waits for them, and re-layouts: 10.8 us -> 1.57 us
    pallas_call x1, Pallas kernels: 70 us -> 63 us  [body(): pl.pallas_call(kernel, out_shape=jax.ShapeDtypeStruct((8, 64, 128), bf16)...]
where the time goes in v2:
time: 66.2 us; the launch traced here: 65.3 us
  Pallas kernels  63 us (95%)
  local copies, waits for them, and re-layouts  1.57 us (2%)
    pallas_call x1, Pallas kernels, body(): pl.pallas_call(kernel, out_shape=jax.ShapeDtypeStruct((8, 64, 128), bf16)...  63 us
    unnamed x1, local copies, waits for them, and re-layouts  1.57 us

profile of v2, /device:TPU:7, one launch (start us, length us, event | category | flops | bytes accessed | tf_op | source)
XLA Modules:
  0.0 65.3 jit_solution(15597632595052954744)
XLA Ops:
  0.7 63.0 %shard_map.109 = bf16[8,64,128]{2,1,0:T(8,128)(2,1)} custom-call(bf16[1,64,128]{2,1,0:T(8,128)(2,1)} %parent_hbm.1, bf16[1,64,128]{2,1,0:T(8,128)(2,1)} %mid_hbm.1, bf16[8,64,128]{2,1,0:T(8,128)(2,1)} %fine_hbm.1, bf16[64,64,189]{2,1,0:T(8,128)(2,1)} %bitcast.2, bf16[64,64,189]{2,1,0:T(8,128)(2,1)} %bitcast.3, bf16[8,64,64]{2,1,0:T(8,128)(2,1)} %shift_hbm.1, ...), custom_call_target="tpu_custom_call" | custom-call | tf_op jit(solution)/shard_map/pallas_call | solution.py:453
  63.7 1.6 %copy.14 = bf16[8,64,128]{2,1,0:T(8,128)(2,1)} copy(bf16[8,64,128]{2,1,0:T(8,128)(2,1)} %shard_map.109) | data formatting | bytes 262144

commit v3 on v2

--- a/solution.py
+++ b/solution.py
@@ -179,11 +179,20 @@
     pl.semaphore_wait(barrier, 8 + (space + 31) // 32 + (62 - space) // 32)
 
     own = owners[OWN]
-    for j in range(8):
-        if j != OWN:
-            o = owners[j]
-            remote(words.at[own], words.at[own], list_send.at[o], list_recv.at[own], peer(o)).start()
-            remote(stage.at[o], raw.at[1, core, own], a2a_send.at[o], a2a_recv.at[own], peer(o)).start()
+    def send_list(o):
+        remote(words.at[own], words.at[own], list_send.at[o], list_recv.at[own], peer(o)).start()
+
+    def send_boxes(o):
+        remote(stage.at[o], raw.at[1, core, own], a2a_send.at[o], a2a_recv.at[own], peer(o)).start()
+
+    for j in range(4):
+        send_list(owners[j])
+    for j in range(4):
+        send_boxes(owners[j])
+    for j in (5, 6, 7):
+        send_boxes(owners[j])
+    for j in (5, 6, 7):
+        send_list(owners[j])
     raw[1, core, own] = stage[own]
 
     def forward(o):
@@ -279,6 +288,9 @@
         arrive(owners[j])
     for j in (4, 5, 6, 7):
         arrive_side(owners[j])
+    for j in range(4):
+        arrive(owners[j])
+
     copies[10].wait()
     operators(ops_fine, w_fine)
 
@@ -314,8 +326,6 @@
     mid_lists = pltpu.make_async_copy(steps_mid, sm_mid, sm_sem.at[STEPS])
     mid_lists.start()
 
-    for j in range(4):
-        arrive(owners[j])
     for j in range(4):
         arrive_side(owners[j])
     for j in (4, 5, 6, 7, 0, 1, 2, 3):

time: 66.2 us -> 64.7 us (0.977)
  Pallas kernels: 63 us -> 61.2 us
    pallas_call x1, Pallas kernels: 63 us -> 61.2 us  [body(): pl.pallas_call(kernel, out_shape=jax.ShapeDtypeStruct((8, 64, 128), bf16)...]
where the time goes in v3:
time: 64.7 us; the launch traced here: 63.4 us
  Pallas kernels  61.2 us (95%)
  local copies, waits for them, and re-layouts  1.57 us (2%)
  between operations  0.66 us (1%)
    pallas_call x1, Pallas kernels, body(): pl.pallas_call(kernel, out_shape=jax.ShapeDtypeStruct((8, 64, 128), bf16)...  61.2 us
    unnamed x1, local copies, waits for them, and re-layouts  1.57 us

profile of v3, /device:TPU:7, one launch (start us, length us, event | category | flops | bytes accessed | tf_op | source)
XLA Modules:
  0.0 63.4 jit_solution(12351137576697226206)
XLA Ops:
  0.7 61.2 %shard_map.109 = bf16[8,64,128]{2,1,0:T(8,128)(2,1)} custom-call(bf16[1,64,128]{2,1,0:T(8,128)(2,1)} %parent_hbm.1, bf16[1,64,128]{2,1,0:T(8,128)(2,1)} %mid_hbm.1, bf16[8,64,128]{2,1,0:T(8,128)(2,1)} %fine_hbm.1, bf16[64,64,189]{2,1,0:T(8,128)(2,1)} %bitcast.2, bf16[64,64,189]{2,1,0:T(8,128)(2,1)} %bitcast.3, bf16[8,64,64]{2,1,0:T(8,128)(2,1)} %shift_hbm.1, ...), custom_call_target="tpu_custom_call" | custom-call | tf_op jit(solution)/shard_map/pallas_call | solution.py:463
  61.9 1.6 %copy.14 = bf16[8,64,128]{2,1,0:T(8,128)(2,1)} copy(bf16[8,64,128]{2,1,0:T(8,128)(2,1)} %shard_map.109) | data formatting | bytes 262144
